TPU v7x, 256 devices: a whole 4x4x8 slice. The times are simulated.
256 devices in a mesh: gx: 4 (over x), gy: 8 (over z), gz: 8 (over y, core).
Axes of the slice: x: 4, y: 4, z: 8, core: 2. Of those that a mesh axis runs over, the one named last changes fastest.
Arguments:
- solution: float32 [4, 8, 32, 64, 1024], P(None, None, 'gx', 'gy', 'gz'), may hold values from -6 to 6
- residual: float32 [4, 8, 32, 64, 1024], P(None, None, 'gx', 'gy', 'gz'), may hold values from -21 to 21
- permeability: float32 [4, 32, 64, 1024], P(None, 'gx', 'gy', 'gz'), may hold values from 0.1 to 1
- storage: float32 [4, 32, 64, 1024], P(None, 'gx', 'gy', 'gz'), may hold values from 0.5 to 2
- tissue_mask: int32 [32, 64, 1024], P('gx', 'gy', 'gz'), may hold values 0 or 1
- tissue_label: int32 [32, 64, 1024], P('gx', 'gy', 'gz'), may hold values from 0 to 2
- exchange_table: float32 [3, 6], replicated, may hold values from 0.2 to 1
Outputs:
- new_solution: float32 [4, 8, 32, 64, 1024], P(None, None, 'gx', 'gy', 'gz')
- new_residual: float32 [4, 8, 32, 64, 1024], P(None, None, 'gx', 'gy', 'gz')
- basis: float32 [4, 32, 32, 64, 1024], P(None, None, 'gx', 'gy', 'gz')
All inputs are finite; a program needn't handle non-finite values. No bound on the sum of `tissue_mask` on one device may be relied on, other than what follows from the above.
Results may differ from a plain program's by a relative error of at most 0.027.
Values sent between devices are 32-bit elements; how exact they have to be, the bound alone decides.
No kernel may reach another device: no remote copies, remote signals or barrier semaphores. Data moves between devices by JAX's collectives and lax.ppermute only.
A program may use at most 128 MiB of HBM per device.

v0:
```python
import jax
import jax.numpy as jnp
import numpy as np
from jax import lax
from jax.sharding import PartitionSpec as P

RHS = 8
S = 4
PAIRS = ((0, 1), (0, 2), (0, 3), (1, 2), (1, 3), (2, 3))
SHIFTS = (2.0, 14.0, 6.0, 10.0)
NEWTON_SCALE = 8.0
HIGHEST_PRECISION = lax.Precision.HIGHEST


def padded(cells, sides, width):
    for axis, dim in sides:
        count = lax.axis_size(axis)
        ends = count - 1
        head = lax.slice_in_dim(cells, 0, width, axis=dim)
        tail = lax.slice_in_dim(cells, cells.shape[dim] - width, cells.shape[dim], axis=dim)
        cells = jnp.concatenate(
            [
                lax.ppermute(tail, axis, [(i, (i + 1) % count) for i in range(ends)]),
                cells,
                lax.ppermute(head, axis, [((i + 1) % count, i) for i in range(ends)]),
            ],
            axis=dim,
        )
    return cells


def shifted(array, direction, offset):
    leading = array.ndim - 3
    index = [slice(None)] * leading
    for dimension in range(3):
        length = array.shape[leading + dimension]
        if dimension == direction:
            index.append(slice(offset, length - 2 + offset))
        else:
            index.append(slice(1, length - 1))
    return array[tuple(index)]


def interior(array):
    return shifted(array, 0, 1)


def stencil(field, perm_pad, mask_pad, store_pad, rate_pad):
    centre = interior(field)
    perm_mid = interior(perm_pad)
    mask_mid = interior(mask_pad)
    result = interior(store_pad)[:, None] * centre
    for direction in range(3):
        for offset in (0, 2):
            faces = (
                0.5
                * (perm_mid + shifted(perm_pad, direction, offset))
                * (mask_mid * shifted(mask_pad, direction, offset))
            )
            result = result + faces[:, None] * (centre - shifted(field, direction, offset))
    rate_mid = interior(rate_pad)
    pieces = [result[number] for number in range(4)]
    for number, pair in enumerate(PAIRS):
        flow = rate_mid[number] * (centre[pair[0]] - centre[pair[1]])
        pieces[pair[0]] = pieces[pair[0]] + flow
        pieces[pair[1]] = pieces[pair[1]] - flow
    return jnp.stack(pieces)


def apply_padded(field_pad, coeff_pad):
    return stencil(field_pad, coeff_pad[0:4], coeff_pad[14], coeff_pad[4:8], coeff_pad[8:14])


def build_coefficients(permeability, storage, tissue_mask, tissue_label, exchange_table):
    mask_float = tissue_mask.astype(jnp.float32)
    rates = jnp.zeros((6,) + tissue_mask.shape, jnp.float32)
    for level in range(3):
        weight = (tissue_label == level).astype(jnp.float32)
        rates = rates + exchange_table[level][:, None, None, None] * weight[None]
    rates = rates * mask_float[None]
    return jnp.concatenate([permeability, storage, rates, mask_float[None]], 0)


def newton_table(steps, rhs_count):
    table = np.zeros(((steps + 1) * rhs_count, steps * rhs_count), np.float32)
    for index in range(steps):
        table[
            index * rhs_count : (index + 1) * rhs_count, index * rhs_count : (index + 1) * rhs_count
        ] = SHIFTS[index] * np.eye(rhs_count)
        table[
            (index + 1) * rhs_count : (index + 2) * rhs_count,
            index * rhs_count : (index + 1) * rhs_count,
        ] = NEWTON_SCALE * np.eye(rhs_count)
    return jnp.asarray(table)


def local_gram(blocks):
    stacked = jnp.stack(blocks)
    flat = stacked.reshape(stacked.shape[0], stacked.shape[1], stacked.shape[2], -1)
    gram = jnp.einsum("kcjm,lcim->kjli", flat, flat, precision=HIGHEST_PRECISION)
    total = stacked.shape[0] * stacked.shape[2]
    return gram.reshape(total, total)


def lower_factor(matrix):
    extent = matrix.shape[0]
    positions = jnp.arange(extent)
    columns = []
    for col_index in range(extent):
        column = matrix[:, col_index]
        for inner in range(col_index):
            column = column - columns[inner] * columns[inner][col_index]
        pivot_value = jnp.sqrt(column[col_index])
        column = jnp.where(positions >= col_index, column / pivot_value, jnp.zeros_like(column))
        columns.append(column)
    return jnp.stack(columns, 1)


def lower_inverse(lower):
    extent = lower.shape[0]
    identity = jnp.eye(extent, dtype=lower.dtype)
    solved_rows = []
    for row_index in range(extent):
        current_row = identity[row_index]
        for inner in range(row_index):
            current_row = current_row - lower[row_index, inner] * solved_rows[inner]
        solved_rows.append(current_row / lower[row_index, row_index])
    return jnp.stack(solved_rows, 0)


def matmul(left, right):
    return jnp.dot(left, right, precision=HIGHEST_PRECISION)


def project(gram, steps, rhs_count):
    width = steps * rhs_count
    table = newton_table(steps, rhs_count)
    leading = gram[:width, :width]
    leading = 0.5 * (leading + leading.T)
    lower_inv = lower_inverse(lower_factor(leading))
    moment = matmul(gram[:width, :], table)
    moment = 0.5 * (moment + moment.T)
    projected = matmul(matmul(lower_inv, moment), lower_inv.T)
    projected = 0.5 * (projected + projected.T)
    right_part = matmul(lower_inv, gram[:width, :rhs_count])
    proj_inv = lower_inverse(lower_factor(projected))
    solved = matmul(proj_inv.T, matmul(proj_inv, right_part))
    inverse = lower_inv.T
    coeff = matmul(inverse, solved)
    extended = matmul(table, coeff)
    return (inverse, coeff, extended)


def finish(solution, residual, blocks, inverse, coeff, extended, steps, rhs_count):
    stacked = jnp.stack(blocks)
    flat = stacked.reshape(stacked.shape[0], stacked.shape[1], stacked.shape[2], -1)
    basis = jnp.einsum(
        "kcjm,kjq->cqm",
        flat[:steps],
        inverse.reshape(steps, rhs_count, -1),
        precision=HIGHEST_PRECISION,
    )
    basis = basis.reshape((stacked.shape[1], steps * rhs_count) + stacked.shape[3:])
    update = jnp.einsum(
        "kcjm,kji->cim",
        flat[:steps],
        coeff.reshape(steps, rhs_count, rhs_count),
        precision=HIGHEST_PRECISION,
    )
    image = jnp.einsum(
        "kcjm,kji->cim",
        flat,
        extended.reshape(steps + 1, rhs_count, rhs_count),
        precision=HIGHEST_PRECISION,
    )
    return (
        solution + update.reshape(solution.shape),
        residual - image.reshape(residual.shape),
        basis,
    )


def body(solution, residual, permeability, storage, tissue_mask, tissue_label, exchange_table):
    coefficients = build_coefficients(
        permeability, storage, tissue_mask, tissue_label, exchange_table
    )
    blocks = [residual]
    coeff_rim = padded(coefficients, (("gx", 1), ("gy", 2), ("gz", 3)), 1)
    current = residual
    for index in range(S):
        field_pad = padded(current, (("gx", 2), ("gy", 3), ("gz", 4)), 1)
        applied = apply_padded(field_pad, coeff_rim)
        current = (applied - SHIFTS[index] * current) / NEWTON_SCALE
        blocks.append(current)
    gram = lax.psum(local_gram(blocks), ("gx", "gy", "gz"))
    inverse, coeff, extended = project(gram, S, RHS)
    return finish(solution, residual, blocks, inverse, coeff, extended, S, RHS)


def solution(mesh):
    return jax.shard_map(
        body,
        mesh=mesh,
        in_specs=(
            P(None, None, "gx", "gy", "gz"),
            P(None, None, "gx", "gy", "gz"),
            P(None, "gx", "gy", "gz"),
            P(None, "gx", "gy", "gz"),
            P("gx", "gy", "gz"),
            P("gx", "gy", "gz"),
            P(),
        ),
        out_specs=(
            P(None, None, "gx", "gy", "gz"),
            P(None, None, "gx", "gy", "gz"),
            P(None, None, "gx", "gy", "gz"),
        ),
        check_vma=False,
    )
```

profile of v0, /device:TPU:1, one launch (start us, length us, event | category | flops | bytes accessed | tf_op | source)
XLA Modules:
  0.0 1804.4 jit_solution(12916086023873227692)
XLA Ops:
  271.1 76.3 %psum.7 = f32[40,40]{1,0:T(8,128)S(1)} all-reduce(f32[40,40]{1,0:T(8,128)S(1)} %fusion.4), channel_id=1, replica_groups=mesh['gx'=4,'gy'=8,'gz'=8] {'gx','gy','gz'}, use_global_device_ids=true, to_apply=%region_0.0 | all-reduce | flops 1600 | bytes 12800 | tf_op jit(solution)/shard_map/psum | solution.py:195
  518.4 11.8 multiply_subtract_fusion.41
  532.2 12.5 multiply_subtract_fusion.40
  546.7 12.9 multiply_subtract_fusion.39
  567.5 13.7 multiply_subtract_fusion.38
  583.1 14.4 multiply_subtract_fusion.37
  599.6 14.9 multiply_subtract_fusion.36
  616.4 15.8 multiply_subtract_fusion.35
  634.2 16.6 multiply_subtract_fusion.34
  652.9 16.6 multiply_subtract_fusion.33
  671.4 17.2 multiply_subtract_fusion.32
  690.8 18.4 %multiply_subtract_fusion.31 = f32[32]{0:T(128)S(1)} fusion(f32[32]{0:T(128)S(1)} %get-tuple-element.34, f32[]{:T(128)} %bitcast.543, f32[]{:T(128)} %bitcast.542, f32[]{:T(128)} %bitcast.541, f32[]{:T(128)} %bitcast.540, f32[]{:T(128)} %bitcast.539, f32[]{:T(128)} %bitcast.538, f32[]{:T(128)} %bitcast.537, f32[]{:T(128)} %bitcast.536, f32[]{:T(128)} %bitcast.535, ...), kind=kLoop, calls=%fused_computation.604 | loop fusion | flops 4608 | bytes 4196 | tf_op jit(solution)/shard_map/sub | solution.py:112
  711.1 19.0 %multiply_subtract_fusion.30 = f32[32]{0:T(128)S(1)} fusion(f32[32]{0:T(128)S(1)} %get-tuple-element.33, f32[]{:T(128)} %bitcast.576, f32[]{:T(128)} %bitcast.575, f32[]{:T(128)} %bitcast.574, f32[]{:T(128)} %bitcast.573, f32[]{:T(128)} %bitcast.572, f32[]{:T(128)} %bitcast.571, f32[]{:T(128)} %bitcast.570, f32[]{:T(128)} %bitcast.569, f32[]{:T(128)} %bitcast.568, ...), kind=kLoop, calls=%fused_computation.602 | loop fusion | flops 4768 | bytes 4332 | tf_op jit(solution)/shard_map/sub | solution.py:112
  731.9 65.1 %subtract_divide_fusion.49 = (f32[1,32]{1,0:T(1,128)S(1)}, f32[1,32]{1,0:T(1,128)S(1)}, f32[1,32]{1,0:T(1,128)S(1)}, f32[1,32]{1,0:T(1,128)S(1)}, f32[1,32]{1,0:...) fusion(f32[32,32]{1,0:T(8,128)S(1)} %fusion.206, ...), kind=kLoop, calls=%fused_computation.639 | loop fusion | flops 6272 | bytes 4004 | tf_op jit(solution)/shard_map/div | solution.py:127
  797.1 137.1 %subtract_divide_fusion.38 = (f32[1,32]{1,0:T(1,128)S(1)}, f32[1,32]{1,0:T(1,128)S(1)}, f32[1,32]{1,0:T(1,128)S(1)}, f32[1,32]{1,0:T(1,128)S(1)}, f32[1,32]{1,0:...) fusion(f32[1,32]{1,0:T(1,128)S(1)} %get-tuple-element.113, ...), kind=kLoop, calls=%fused_computation.617 | loop fusion | flops 13728 | bytes 5488 | tf_op jit(solution)/shard_map/div | solution.py:127
  934.2 127.1 %subtract_divide_fusion.31 = (f32[1,32]{1,0:T(1,128)S(1)}, f32[1,32]{1,0:T(1,128)S(1)}, f32[1,32]{1,0:T(1,128)S(1)}, f32[1,32]{1,0:T(1,128)S(1)}, f32[1,32]{1,0:...) fusion(f32[1,32]{1,0:T(1,128)S(1)} %get-tuple-element.102, f32[1,32]{1,0:T(1,128)S(1)} %get-tuple-element.103, ...), kind=kLoop, calls=%fused_computation.603 | loop fusion | flops 12768 | bytes 5804 | tf_op jit(solution)/shard_map/div | solution.py:127
  1232.8 11.8 multiply_subtract_fusion.11
  1246.6 12.5 multiply_subtract_fusion.10
  1261.1 12.9 multiply_subtract_fusion.9
  1281.9 13.7 multiply_subtract_fusion.8
  1297.5 14.4 multiply_subtract_fusion.7
  1314.0 14.9 multiply_subtract_fusion.6
  1330.8 15.8 multiply_subtract_fusion.5
  1348.7 16.6 multiply_subtract_fusion.4
  1367.3 16.6 multiply_subtract_fusion.3
  1385.8 17.2 multiply_subtract_fusion.2
  1405.2 18.4 %multiply_subtract_fusion.1 = f32[32]{0:T(128)S(1)} fusion(f32[32]{0:T(128)S(1)} %get-tuple-element.4, f32[]{:T(128)} %bitcast.1105, f32[]{:T(128)} %bitcast.1104, f32[]{:T(128)} %bitcast.1103, f32[]{:T(128)} %bitcast.1102, f32[]{:T(128)} %bitcast.1101, f32[]{:T(128)} %bitcast.1100, f32[]{:T(128)} %bitcast.1099, f32[]{:T(128)} %bitcast.1098, f32[]{:T(128)} %bitcast.1097, ...), kind=kLoop, calls=%fused_computation.543 | loop fusion | flops 4608 | bytes 4196 | tf_op jit(solution)/shard_map/sub | solution.py:112
  1425.5 19.0 %multiply_subtract_fusion = f32[32]{0:T(128)S(1)} fusion(f32[32]{0:T(128)S(1)} %get-tuple-element.3, f32[]{:T(128)} %bitcast.1138, f32[]{:T(128)} %bitcast.1137, f32[]{:T(128)} %bitcast.1136, f32[]{:T(128)} %bitcast.1135, f32[]{:T(128)} %bitcast.1134, f32[]{:T(128)} %bitcast.1133, f32[]{:T(128)} %bitcast.1132, f32[]{:T(128)} %bitcast.1131, f32[]{:T(128)} %bitcast.1130, ...), kind=kLoop, calls=%fused_computation.541 | loop fusion | flops 4768 | bytes 4332 | tf_op jit(solution)/shard_map/sub | solution.py:112
  1446.3 65.1 %subtract_divide_fusion.18 = (f32[1,32]{1,0:T(1,128)S(1)}, f32[1,32]{1,0:T(1,128)S(1)}, f32[1,32]{1,0:T(1,128)S(1)}, f32[1,32]{1,0:T(1,128)S(1)}, f32[1,32]{1,0:...) fusion(f32[32,32]{1,0:T(8,128)S(1)} %fusion.206, ...), kind=kLoop, calls=%fused_computation.578 | loop fusion | flops 6272 | bytes 4004 | tf_op jit(solution)/shard_map/div | solution.py:127
  1511.5 137.1 %subtract_divide_fusion.7 = (f32[1,32]{1,0:T(1,128)S(1)}, f32[1,32]{1,0:T(1,128)S(1)}, f32[1,32]{1,0:T(1,128)S(1)}, f32[1,32]{1,0:T(1,128)S(1)}, f32[1,32]{1,0:T...) fusion(f32[1,32]{1,0:T(1,128)S(1)} %get-tuple-element.81, ...), kind=kLoop, calls=%fused_computation.556 | loop fusion | flops 13728 | bytes 5488 | tf_op jit(solution)/shard_map/div | solution.py:127
  1648.6 127.1 %subtract_divide_fusion = (f32[1,32]{1,0:T(1,128)S(1)}, f32[1,32]{1,0:T(1,128)S(1)}, f32[1,32]{1,0:T(1,128)S(1)}, f32[1,32]{1,0:T(1,128)S(1)}, f32[1,32]{1,0:T(1...) fusion(f32[1,32]{1,0:T(1,128)S(1)} %get-tuple-element.70, f32[1,32]{1,0:T(1,128)S(1)} %get-tuple-element.71, ...), kind=kLoop, calls=%fused_computation.542 | loop fusion | flops 12768 | bytes 5804 | tf_op jit(solution)/shard_map/div | solution.py:127
  1776.6 11.7 fusion.131
  (587 shorter events, 643.0 us)
Async XLA Ops:
  3.9 17.9 collective-permute-start
  8.0 13.8 collective-permute-start.1
  10.0 18.1 %collective-permute-start.7 = (f32[4,8,1,8,128]{4,1,3,2,0:T(8,128)S(1)}, f32[4,8,1,8,128]{4,1,3,2,0:T(8,128)S(1)}, u32[]{:S(2)}, u32[]{:S(2)}) collective-permute-start(f32[4,8,1,8,128]{4,1,3,2,0:T(8,128)S(1)} %get-tuple-element.169), channel_id=1, source_target_pairs={{64,0},{128,64},{192,128},{65,1},{129,65},{193,129},{66,2},{130,66... | collective-permute-start | bytes 393224 | tf_op jit(solution)/shard_map/ppermute | solution.py:25
  11.3 16.1 collective-permute-start.6
  16.6 74.7 %copy-start.40 = (f32[8,8,128]{2,1,0:T(8,128)}, f32[8,8,128]{2,1,0:T(8,128)S(1)}, u32[]{:S(2)}) copy-start(f32[8,8,128]{2,1,0:T(8,128)S(1)} %get-tuple-element.185) | copy-start | bytes 98308
  21.9 6.2 collective-permute-start.3
  23.2 5.6 collective-permute-start.2
  36.0 17.0 collective-permute-start.5
  40.1 10.8 collective-permute-start.4
  44.9 14.5 collective-permute-start.8
  49.6 9.8 collective-permute-start.9
  71.0 12.2 collective-permute-start.11
  73.0 6.2 collective-permute-start.10
  92.8 5.8 collective-permute-start.12
  96.5 6.3 collective-permute-start.13
  102.8 7.7 collective-permute-start.14
  106.8 8.3 collective-permute-start.15
  121.4 9.9 collective-permute-start.16
  129.4 6.6 collective-permute-start.17
  147.9 5.8 collective-permute-start.18
  151.0 5.9 collective-permute-start.19
  157.0 7.8 collective-permute-start.20
  162.2 7.6 collective-permute-start.21
  180.9 15.0 collective-permute-start.23
  182.9 9.0 collective-permute-start.22
  205.7 3.9 collective-permute-start.24
  207.3 5.7 collective-permute-start.25
  213.0 7.2 collective-permute-start.26
  217.9 6.1 collective-permute-start.27
  235.1 15.8 collective-permute-start.29
  237.1 9.8 collective-permute-start.28
  262.7 169.8 %copy-start.77 = (f32[40,32]{1,0:T(8,128)S(1)}, f32[40,32]{1,0:T(8,128)}, u32[]{:S(2)}) copy-start(f32[40,32]{1,0:T(8,128)} %constant.92.clone) | copy-start | bytes 15364
  (76 other events, 782.7 us)
where the time goes:
time: 1830 us; the launch traced here: 1800 us
  other arithmetic  1320 us (72%)
  local copies, waits for them, and re-layouts  207 us (11%)
  starting transfers between devices  90.5 us (5%)
  blocking collectives  76.3 us (4%)
  between operations  47.1 us (3%)
  waiting for transfers between devices  34.7 us (2%)
  matrix products  32.4 us (2%)
    div x6, other arithmetic, lower_inverse(): solved_rows.append(current_row / lower[row_index, row_index])  659 us
    sub x68, other arithmetic, lower_factor(): column = column - columns[inner] * columns[inner][col_index]  621 us
    psum x1, blocking collectives, body(): gram = lax.psum(local_gram(blocks), ('gx', 'gy', 'gz'))  76.3 us
    ppermute x15, starting transfers between devices, padded(): lax.ppermute(tail, axis, [(i, (i + 1) % count) for i in range(ends)])  65.7 us
    slice x64, local copies, waits for them, and re-layouts, lower_factor(): pivot_value = jnp.sqrt(column[col_index])  39.9 us
    slice x54, local copies, waits for them, and re-layouts, lower_inverse(): current_row = current_row - lower[row_index, inner] * solved_rows[inner]  38.3 us
  transfers between devices with their start and end apart: 30, of which 14 were waited for; matrix products, arithmetic and copies ran while one was open for 2% of the time, Pallas kernels for 0%

commit v1 on v0

--- a/solution.py
+++ b/solution.py
@@ -192,7 +192,7 @@
         applied = apply_padded(field_pad, coeff_rim)
         current = (applied - SHIFTS[index] * current) / NEWTON_SCALE
         blocks.append(current)
-    gram = lax.psum(local_gram(blocks), ("gx", "gy", "gz"))
+    gram = jax.lax.psum(jax.lax.psum(local_gram(blocks), axis_name=("gy", "gz")), axis_name="gx")
     inverse, coeff, extended = project(gram, S, RHS)
     return finish(solution, residual, blocks, inverse, coeff, extended, S, RHS)
 

time: 1830 us -> 2010 us (1.098)
  blocking collectives: 76.3 us -> 252 us
    psum x1 -> x2, blocking collectives: 76.3 us -> 252 us  [the longest x1 241 us: body(): jax.lax.psum(local_gram(blocks), axis_name=('gy', 'gz'))]
where the time goes in v1:
time: 2010 us; the launch traced here: 1980 us
  other arithmetic  1320 us (66%)
  blocking collectives  252 us (13%)
  local copies, waits for them, and re-layouts  207 us (10%)
  starting transfers between devices  90.4 us (4%)
  between operations  47.2 us (2%)
  waiting for transfers between devices  34.7 us (2%)
  matrix products  32.4 us (2%)
    div x6, other arithmetic, lower_inverse(): solved_rows.append(current_row / lower[row_index, row_index])  659 us
    sub x68, other arithmetic, lower_factor(): column = column - columns[inner] * columns[inner][col_index]  621 us
    psum x1, blocking collectives, body(): jax.lax.psum(local_gram(blocks), axis_name=('gy', 'gz'))  241 us
    ppermute x15, starting transfers between devices, padded(): lax.ppermute(tail, axis, [(i, (i + 1) % count) for i in range(ends)])  65.7 us
  transfers between devices with their start and end apart: 30, of which 14 were waited for; matrix products, arithmetic and copies ran while one was open for 2% of the time, Pallas kernels for 0%

profile of v1, /device:TPU:1, one launch (start us, length us, event | category | flops | bytes accessed | tf_op | source)
XLA Modules:
  0.0 1980.2 jit_solution(7008119767997113431)
XLA Ops:
  271.1 241.0 %psum.14 = f32[40,40]{1,0:T(8,128)S(1)} all-reduce(f32[40,40]{1,0:T(8,128)S(1)} %fusion.4), channel_id=1, replica_groups=mesh['gx'=4,'gy'=8,'gz'=8] {'gy','gz'}, use_global_device_ids=true, to_apply=%region_0.0 | all-reduce | flops 1600 | bytes 12800 | tf_op jit(solution)/shard_map/psum | solution.py:195
  694.0 11.8 multiply_subtract_fusion.41
  707.9 12.6 multiply_subtract_fusion.40
  722.5 13.1 multiply_subtract_fusion.39
  743.7 13.8 multiply_subtract_fusion.38
  759.6 14.7 multiply_subtract_fusion.37
  776.2 14.8 multiply_subtract_fusion.36
  792.9 15.4 multiply_subtract_fusion.35
  810.3 16.5 multiply_subtract_fusion.34
  828.8 16.9 multiply_subtract_fusion.33
  847.5 17.4 multiply_subtract_fusion.32
  866.9 18.2 multiply_subtract_fusion.31
  887.2 18.9 multiply_subtract_fusion.30
  907.9 65.3 %subtract_divide_fusion.49 = (f32[1,32]{1,0:T(1,128)S(1)}, f32[1,32]{1,0:T(1,128)S(1)}, f32[1,32]{1,0:T(1,128)S(1)}, f32[1,32]{1,0:T(1,128)S(1)}, f32[1,32]{1,0:...) fusion(f32[32,32]{1,0:T(8,128)S(1)} %fusion.206, ...), kind=kLoop, calls=%fused_computation.639 | loop fusion | flops 6272 | bytes 4004 | tf_op jit(solution)/shard_map/div | solution.py:127
  973.2 137.1 %subtract_divide_fusion.38 = (f32[1,32]{1,0:T(1,128)S(1)}, f32[1,32]{1,0:T(1,128)S(1)}, f32[1,32]{1,0:T(1,128)S(1)}, f32[1,32]{1,0:T(1,128)S(1)}, f32[1,32]{1,0:...) fusion(f32[1,32]{1,0:T(1,128)S(1)} %get-tuple-element.113, ...), kind=kLoop, calls=%fused_computation.617 | loop fusion | flops 13728 | bytes 5488 | tf_op jit(solution)/shard_map/div | solution.py:127
  1110.3 126.8 %subtract_divide_fusion.31 = (f32[1,32]{1,0:T(1,128)S(1)}, f32[1,32]{1,0:T(1,128)S(1)}, f32[1,32]{1,0:T(1,128)S(1)}, f32[1,32]{1,0:T(1,128)S(1)}, f32[1,32]{1,0:...) fusion(f32[1,32]{1,0:T(1,128)S(1)} %get-tuple-element.102, f32[1,32]{1,0:T(1,128)S(1)} %get-tuple-element.103, ...), kind=kLoop, calls=%fused_computation.603 | loop fusion | flops 12768 | bytes 5804 | tf_op jit(solution)/shard_map/div | solution.py:127
  1408.3 11.8 multiply_subtract_fusion.11
  1422.2 12.6 multiply_subtract_fusion.10
  1436.8 13.1 multiply_subtract_fusion.9
  1458.0 13.8 multiply_subtract_fusion.8
  1473.9 14.7 multiply_subtract_fusion.7
  1490.5 14.8 multiply_subtract_fusion.6
  1507.2 15.4 multiply_subtract_fusion.5
  1524.6 16.5 multiply_subtract_fusion.4
  1543.1 16.9 multiply_subtract_fusion.3
  1561.8 17.4 multiply_subtract_fusion.2
  1581.2 18.2 multiply_subtract_fusion.1
  1601.5 18.9 multiply_subtract_fusion
  1622.2 65.3 %subtract_divide_fusion.18 = (f32[1,32]{1,0:T(1,128)S(1)}, f32[1,32]{1,0:T(1,128)S(1)}, f32[1,32]{1,0:T(1,128)S(1)}, f32[1,32]{1,0:T(1,128)S(1)}, f32[1,32]{1,0:...) fusion(f32[32,32]{1,0:T(8,128)S(1)} %fusion.206, ...), kind=kLoop, calls=%fused_computation.578 | loop fusion | flops 6272 | bytes 4004 | tf_op jit(solution)/shard_map/div | solution.py:127
  1687.5 137.1 %subtract_divide_fusion.7 = (f32[1,32]{1,0:T(1,128)S(1)}, f32[1,32]{1,0:T(1,128)S(1)}, f32[1,32]{1,0:T(1,128)S(1)}, f32[1,32]{1,0:T(1,128)S(1)}, f32[1,32]{1,0:T...) fusion(f32[1,32]{1,0:T(1,128)S(1)} %get-tuple-element.81, ...), kind=kLoop, calls=%fused_computation.556 | loop fusion | flops 13728 | bytes 5488 | tf_op jit(solution)/shard_map/div | solution.py:127
  1824.6 126.8 %subtract_divide_fusion = (f32[1,32]{1,0:T(1,128)S(1)}, f32[1,32]{1,0:T(1,128)S(1)}, f32[1,32]{1,0:T(1,128)S(1)}, f32[1,32]{1,0:T(1,128)S(1)}, f32[1,32]{1,0:T(1...) fusion(f32[1,32]{1,0:T(1,128)S(1)} %get-tuple-element.70, f32[1,32]{1,0:T(1,128)S(1)} %get-tuple-element.71, ...), kind=kLoop, calls=%fused_computation.542 | loop fusion | flops 12768 | bytes 5804 | tf_op jit(solution)/shard_map/div | solution.py:127
  1952.4 11.7 fusion.131
  (588 shorter events, 653.4 us)
Async XLA Ops:
  3.9 17.9 collective-permute-start
  8.0 13.8 collective-permute-start.1
  10.0 18.1 collective-permute-start.7
  11.3 16.1 collective-permute-start.6
  16.6 74.7 %copy-start.40 = (f32[8,8,128]{2,1,0:T(8,128)}, f32[8,8,128]{2,1,0:T(8,128)S(1)}, u32[]{:S(2)}) copy-start(f32[8,8,128]{2,1,0:T(8,128)S(1)} %get-tuple-element.185) | copy-start | bytes 98308
  21.9 6.2 collective-permute-start.3
  23.2 5.6 collective-permute-start.2
  36.0 16.9 collective-permute-start.5
  40.1 10.8 collective-permute-start.4
  44.9 14.4 collective-permute-start.8
  49.6 9.8 collective-permute-start.9
  71.0 12.2 collective-permute-start.11
  72.9 6.2 collective-permute-start.10
  92.8 5.8 collective-permute-start.12
  96.4 6.3 collective-permute-start.13
  102.8 7.7 collective-permute-start.14
  106.8 8.3 collective-permute-start.15
  121.4 9.9 collective-permute-start.16
  129.4 6.6 collective-permute-start.17
  147.9 5.8 collective-permute-start.18
  151.0 5.9 collective-permute-start.19
  156.9 7.8 collective-permute-start.20
  162.2 7.6 collective-permute-start.21
  180.9 15.0 collective-permute-start.23
  182.8 9.0 collective-permute-start.22
  205.7 4.0 collective-permute-start.24
  207.3 5.7 collective-permute-start.25
  213.0 7.2 collective-permute-start.26
  217.9 6.1 collective-permute-start.27
  235.2 15.8 collective-permute-start.29
  237.1 9.8 collective-permute-start.28
  262.8 345.6 %copy-start.77 = (f32[40,32]{1,0:T(8,128)S(1)}, f32[40,32]{1,0:T(8,128)}, u32[]{:S(2)}) copy-start(f32[40,32]{1,0:T(8,128)} %constant.92.clone) | copy-start | bytes 15364
  (76 other events, 782.4 us)
